TPU v7x, 32 devices: a whole 2x2x4 slice. The times are simulated.
32 devices in a mesh: rad: 4 (over y, x), azi: 8 (over z, core).
Axes of the slice: x: 2, y: 2, z: 4, core: 2. Of those that a mesh axis runs over, the one named last changes fastest.
Arguments:
- relative_base_heat: float32 [64, 256, 512], P('rad', 'azi'), may hold values from 0.75 to 1.25
- base_deformation_size: float32 [64, 256, 512], P('rad', 'azi'), may hold values from 0.25 to 1
- base_streamwise_flux: float32 [64, 256, 512], P('rad', 'azi'), may hold values from 0.2 to 1
- goal_heat_change: float32 [64, 256, 512], P('rad', 'azi'), may hold values from 0.25 to 2
- initial_costate_heat: float32 [64, 256, 512], P('rad', 'azi'), may hold values from 0.2 to 2
Outputs:
- temperature_adjoint: float32 [64, 256, 512], P('rad', 'azi')
- lengthwise_velocity_sensitivity: float32 [64, 256, 512], P('rad', 'azi')
All inputs are finite; a program needn't handle non-finite values.
Results may differ from a plain program's by a relative error of at most 0.00045.
Values sent between devices are 32-bit elements; how exact they have to be, the bound alone decides.
A program may use at most 128 MiB of HBM per device.

v0:
```python
import functools

import jax
import jax.numpy as jnp
from jax import lax
from jax.experimental import pallas as pl
from jax.experimental.pallas import tpu as pltpu
from jax.sharding import PartitionSpec as P

radial_weight = 8.0
azimuth_weight = 0.25
axial_weight = 0.25
flow_weight = 0.5
mass_weight = 1.0
heat_weight = 0.25
arrhenius_exponent = 2.0
slope_weight = 2.0

MESH = pl.DeviceIdType.MESH
LANES = 128
SUB = 8


def kernel(
    segments,
    sectors,
    heat_hbm,
    size_hbm,
    flux_hbm,
    goal_hbm,
    start_hbm,
    adjoint_hbm,
    sens_hbm,
    heat,
    size,
    flux,
    goal,
    state,
    inv,
    qa,
    rb,
    rhs,
    part,
    out_x,
    out_s,
    halo_out,
    halo_in,
    coef_out,
    coef_in,
    u_out,
    u_in,
    ret_out,
    ret_in,
    factor,
    side_a,
    side_b,
    in_sem,
    out_sem,
    halo_ssem,
    halo_rsem,
    coef_ssem,
    coef_rsem,
    u_ssem,
    u_rsem,
    ret_ssem,
    ret_rsem,
):
    rows, width, axial = heat.shape
    groups = width // SUB
    chunks = axial // LANES
    per_chunk = segments // chunks
    tile_rows = width // (2 * per_chunk)
    inner, outer = tuple(range(1, groups - 1)), (0, groups - 1)
    halves = (inner, outer)
    total = rows * segments
    stiffness = radial_weight * rows * rows

    seg = lax.axis_index("rad")
    sec = lax.axis_index("azi")
    above = lax.rem(sec + 1, sectors)
    below = lax.rem(sec + sectors - 1, sectors)
    peers = [lax.rem(seg + k, segments) for k in range(1, segments)]
    first = seg * rows

    span = rows // 2
    loads = [
        [
            pltpu.make_async_copy(
                src.at[pl.ds(part_of * span, span)],
                dst.at[pl.ds(part_of * span, span)],
                in_sem.at[n, part_of],
            )
            for part_of in range(2)
        ]
        for n, (src, dst) in enumerate(
            (
                (start_hbm, state),
                (heat_hbm, heat),
                (size_hbm, size),
                (flux_hbm, flux),
                (goal_hbm, goal),
            )
        )
    ]
    for load in loads:
        for copy in load:
            copy.start()

    def await_load(load):
        for copy in load:
            copy.wait()

    barrier = pltpu.get_barrier_semaphore()
    for peer in peers:
        pl.semaphore_signal(barrier, inc=1, device_id=(peer, sec), device_id_type=MESH)
    for near in (above, below):
        pl.semaphore_signal(barrier, inc=1, device_id=(seg, near), device_id_type=MESH)

    def halo_copies(sweep):
        return [
            pltpu.make_async_remote_copy(
                src_ref=halo_out.at[sweep, side],
                dst_ref=halo_in.at[sweep, side],
                send_sem=halo_ssem.at[sweep, side],
                recv_sem=halo_rsem.at[sweep, side],
                device_id=(seg, near),
                device_id_type=MESH,
            )
            for side, near in ((0, above), (1, below))
        ]

    def sends(src, dst, ssem, rsem):
        return [
            pltpu.make_async_remote_copy(
                src_ref=src.at[peer],
                dst_ref=dst.at[seg],
                send_sem=ssem.at[peer],
                recv_sem=rsem.at[seg],
                device_id=(peer, sec),
                device_id_type=MESH,
            )
            for peer in peers
        ]

    def await_from(src, dst, ssem, rsem):
        for peer in peers:
            pltpu.make_async_remote_copy(
                src_ref=src.at[peer],
                dst_ref=dst.at[peer],
                send_sem=ssem.at[peer],
                recv_sem=rsem.at[peer],
                device_id=(peer, sec),
                device_id_type=MESH,
            ).wait_recv()

    def geometry(i):
        row = (first + i).astype(jnp.float32)
        radius = 1.0 + (row + 0.5) * (1.0 / total)
        low = stiffness * (1.0 + row * (1.0 / total))
        high = stiffness * (1.0 + (row + 1.0) * (1.0 / total))
        return radius, low, high

    def azimuth_coef(radius):
        return azimuth_weight / jnp.full((1, LANES), radius, jnp.float32)

    def wide(line):
        return jnp.concatenate([line] * chunks, axis=1)

    await_load(loads[0])

    def pack(i, carry):
        halo_out[0, 0, pl.ds(i, 1), :] = state[i, width - 1 : width, :]
        halo_out[0, 1, pl.ds(i, 1), :] = state[i, 0:1, :]
        return carry

    lax.fori_loop(0, rows, pack, 0, unroll=4)
    pl.semaphore_wait(barrier, segments + 1)
    halos = halo_copies(0)
    for copy in halos:
        copy.start()

    for load in loads[1:4]:
        await_load(load)

    def rows_of(g):
        return slice(g * SUB, (g + 1) * SUB)

    def pieces():
        for c in range(chunks):
            for k in range(per_chunk):
                where_rows = slice(k * tile_rows, (k + 1) * tile_rows)
                where_cols = slice(c * LANES, (c + 1) * LANES)
                yield c * per_chunk + k, where_rows, where_cols

    def scatter(slot, plane, c_first, c_last):
        for n, chosen in enumerate(halves):
            lines = jnp.concatenate([plane[rows_of(g)] for g in chosen], axis=0)
            for owner, where_rows, cols in pieces():
                if c_first * LANES <= cols.start < c_last * LANES:
                    at = cols.start - c_first * LANES
                    coef_out[owner, slot, n] = lines[where_rows, at : at + LANES]

    half = 2 * LANES
    for h in range(axial // half):
        cols = slice(h * half, (h + 1) * half)

        def eliminate(i, carry):
            ratio, ea, prod, va, _ = carry
            radius, low, high = geometry(i)
            az2 = 2.0 * azimuth_coef(radius)
            az2 = jnp.concatenate([az2, az2], axis=1)
            viscosity = jnp.exp(
                arrhenius_exponent - arrhenius_exponent * heat[i, :, cols]
            )
            extent = size[i, :, cols]
            shear = (heat_weight * arrhenius_exponent) * viscosity * extent
            ahead = radius * (axial_weight + flow_weight * flux[i, :, cols])
            excess = (
                ahead + radius * (shear * extent + (mass_weight + axial_weight)) + az2
            )
            top = low * ratio + excess
            inverse = 1.0 / (top + high)
            ratio = top * inverse
            ea = (low * inverse) * ea
            upper = high * inverse
            va = va + prod * ea
            prod = prod * upper
            flux[i, :, cols] = ahead
            size[i, :, cols] = shear
            inv[i, :, cols] = inverse
            qa[i, :, cols] = ea
            return ratio, ea, prod, va, upper

        one = jnp.ones((width, half), jnp.float32)
        zero = jnp.zeros((width, half), jnp.float32)
        _, ea, _, va, upper = lax.fori_loop(
            0, rows, eliminate, (one, one, one, zero, zero), unroll=4
        )
        scatter(0, va, 2 * h, 2 * h + 2)
        scatter(1, ea, 2 * h, 2 * h + 2)
        scatter(2, upper, 2 * h, 2 * h + 2)

    coef_sends = sends(coef_out, coef_in, coef_ssem, coef_rsem)
    for copy in coef_sends:
        copy.start()
    coef_in[seg] = coef_out[seg]

    def respond(n, carry):
        q_next, r_next = carry
        i = rows - 1 - n
        _, _, high = geometry(i)
        upper = high * inv[i]
        q_next = qa[i] + upper * q_next
        r_next = upper * r_next
        qa[i] = q_next
        rb[i] = r_next
        return q_next, r_next

    lax.fori_loop(
        0,
        rows,
        respond,
        (jnp.zeros((width, axial), jnp.float32), jnp.ones((width, axial), jnp.float32)),
        unroll=4,
    )

    await_load(loads[4])
    sub = lax.broadcasted_iota(jnp.int32, (SUB, axial), 0)
    lane = lax.broadcasted_iota(jnp.int32, (SUB, axial), 1)

    def right_side(sweep, half):
        chosen = halves[half]

        def step(i, carry):
            radius, _, _ = geometry(i)
            az = wide(azimuth_coef(radius))
            rolled_up, rolled_down, new = {}, {}, []

            def block(g):
                return state[i, g * SUB : (g + 1) * SUB, :]

            def up(g):
                if g < 0:
                    return jnp.broadcast_to(
                        halo_in[sweep, 0, pl.ds(i, 1), :], (SUB, axial)
                    )
                if g not in rolled_up:
                    rolled_up[g] = pltpu.roll(block(g), 1, 0)
                return rolled_up[g]

            def down(g):
                if g >= groups:
                    return jnp.broadcast_to(
                        halo_in[sweep, 1, pl.ds(i, 1), :], (SUB, axial)
                    )
                if g not in rolled_down:
                    rolled_down[g] = pltpu.roll(block(g), SUB - 1, 0)
                return rolled_down[g]

            for g, (u_first, u_last) in zip(chosen, carry):
                here = slice(g * SUB, (g + 1) * SUB)
                x = block(g)
                sides = jnp.where(sub == 0, up(g - 1), up(g)) + jnp.where(
                    sub == SUB - 1, down(g + 1), down(g)
                )
                before = jnp.where(lane == 0, 0.0, pltpu.roll(x, 1, 1))
                after = jnp.where(lane == axial - 1, 0.0, pltpu.roll(x, axial - 1, 1))
                value = (
                    radius * (goal[i, here, :] + mass_weight * x + axial_weight * before)
                    + flux[i, here, :] * after
                    + az * sides
                )
                rhs[i, here, :] = value
                new.append(
                    (u_first + qa[i, here, :] * value, u_last + rb[i, here, :] * value)
                )
            return tuple(new)

        zero = jnp.zeros((SUB, axial), jnp.float32)
        sums = lax.fori_loop(0, rows, step, tuple((zero, zero) for _ in chosen), unroll=2)
        for slot in range(2):
            lines = jnp.concatenate([pair[slot] for pair in sums], axis=0)
            for owner, where_rows, cols in pieces():
                u_out[sweep, half, owner, slot] = lines[where_rows, cols]

    def send_ends(sweep, half):
        at = (sweep, half)
        copies = sends(u_out.at[at], u_in.at[at], u_ssem.at[at], u_rsem.at[at])
        for copy in copies:
            copy.start()
        u_in[sweep, half, seg] = u_out[sweep, half, seg]
        return copies

    def await_ends(sweep, half):
        at = (sweep, half)
        await_from(u_out.at[at], u_in.at[at], u_ssem.at[at], u_rsem.at[at])

    def substitute(half):
        chosen = halves[half]

        def forward(i, carry):
            _, low, _ = geometry(i)
            new = []
            for g, before in zip(chosen, carry):
                here = rows_of(g)
                now = inv[i, here, :] * (rhs[i, here, :] + low * before)
                rhs[i, here, :] = now
                new.append(now)
            return tuple(new)

        def backward(n, carry):
            i = rows - 1 - n
            _, _, high = geometry(i)
            new = []
            for g, after in zip(chosen, carry):
                here = rows_of(g)
                now = rhs[i, here, :] + (high * inv[i, here, :]) * after
                part[i, here, :] = now
                new.append(now)
            return tuple(new)

        zero = tuple(jnp.zeros((SUB, axial), jnp.float32) for _ in chosen)
        lax.fori_loop(0, rows, forward, zero, unroll=4)
        lax.fori_loop(0, rows, backward, zero, unroll=4)

    def reduced_factors(half):
        beta = None
        for s in range(segments):
            v_first, v_last, w_last = [coef_in[s, slot, half] for slot in range(3)]
            w_first = v_last * ((segments + s + 1.0) / (segments + s))
            if s == 0:
                beta = w_last
                factor[half, s, 3] = beta
                continue
            scale = 1.0 / (1.0 - v_first * beta)
            q = scale * w_first
            cross = v_last * beta
            beta = w_last + cross * q
            for slot, plane in enumerate((scale, scale * v_first, q, beta, cross)):
                factor[half, s, slot] = plane

    def reduced_solve(sweep, half):
        firsts, lasts = [], []
        for s in range(segments):
            end = [u_in[sweep, half, s, slot] for slot in range(2)]
            u_first = end[0] * (segments / (stiffness * (segments + s)))
            u_last = end[1] * (segments / (stiffness * (segments + s + 1)))
            if s == 0:
                firsts.append(u_first)
                lasts.append(u_last)
                continue
            p = factor[half, s, 0] * u_first + factor[half, s, 1] * lasts[s - 1]
            firsts.append(p)
            lasts.append(
                u_last + coef_in[s, 1, half] * lasts[s - 1] + factor[half, s, 4] * p
            )
        beyond = jnp.zeros((tile_rows, LANES), jnp.float32)
        ret_out[sweep, half, 0, 0] = beyond
        for s in range(segments - 1, -1, -1):
            ret_out[sweep, half, s, 1] = beyond
            if s < segments - 1:
                ret_out[sweep, half, s + 1, 0] = lasts[s] + factor[half, s, 3] * beyond
            if s > 0:
                beyond = firsts[s] + factor[half, s, 2] * beyond

    def send_back(sweep, half):
        at = (sweep, half)
        copies = sends(ret_out.at[at], ret_in.at[at], ret_ssem.at[at], ret_rsem.at[at])
        for copy in copies:
            copy.start()
        ret_in[sweep, half, seg] = ret_out[sweep, half, seg]
        return copies

    def ends(sweep, half):
        at = (sweep, half)
        await_from(ret_out.at[at], ret_in.at[at], ret_ssem.at[at], ret_rsem.at[at])
        for owner, where_rows, cols in pieces():
            side_a[half, where_rows, cols] = ret_in[sweep, half, owner, 0]
            side_b[half, where_rows, cols] = ret_in[sweep, half, owner, 1]
        return [
            (side_a[half, rows_of(n), :], side_b[half, rows_of(n), :])
            for n in range(len(halves[half]))
        ]

    def solved(i, half, sides):
        for g, (a, b) in zip(halves[half], sides):
            here = rows_of(g)
            yield g, part[i, here, :] + qa[i, here, :] * a + rb[i, here, :] * b

    for copy in halos:
        copy.wait_recv()
    started = [coef_sends, halos]
    for half in (1, 0):
        right_side(0, half)
        started.append(send_ends(0, half))
    await_from(coef_out, coef_in, coef_ssem, coef_rsem)
    for half in (1, 0):
        reduced_factors(half)
    for half in (1, 0):
        substitute(half)
        await_ends(0, half)
        reduced_solve(0, half)
        started.append(send_back(0, half))

    last_lane = lax.broadcasted_iota(jnp.int32, (width, axial), 1) == axial - 1

    def slope(i, carry):
        here = heat[i]
        rise = jnp.where(last_lane, 0.0, pltpu.roll(here, axial - 1, 1) - here)
        heat[i] = slope_weight * rise - size[i]
        return carry

    lax.fori_loop(0, rows, slope, 0, unroll=4)

    for half in (1, 0):
        sides = ends(0, half)

        def advance(i, carry):
            for g, x in solved(i, half, sides):
                state[i, rows_of(g), :] = x
                if g == groups - 1:
                    halo_out[1, 0, pl.ds(i, 1), :] = x[SUB - 1 : SUB, :]
                if g == 0:
                    halo_out[1, 1, pl.ds(i, 1), :] = x[0:1, :]
            return carry

        lax.fori_loop(0, rows, advance, 0, unroll=4)
        if half == 1:
            halos = halo_copies(1)
            started.append(halos)
            for copy in halos:
                copy.start()

    for half in (0, 1):
        if half == 1:
            for copy in halos:
                copy.wait_recv()
        right_side(1, half)
        started.append(send_ends(1, half))
    for half in (0, 1):
        substitute(half)
        await_ends(1, half)
        reduced_solve(1, half)
        started.append(send_back(1, half))

    stores = []
    for half in (0, 1):
        sides = ends(1, half)

        def finish(i, carry):
            for g, x in solved(i, half, sides):
                here = rows_of(g)
                out_x[i, here, :] = x
                out_s[i, here, :] = x * heat[i, here, :]
            return carry

        lax.fori_loop(0, rows, finish, 0, unroll=4)
        for g in halves[half]:
            here = pl.ds(g * SUB, SUB)
            for m, (src, dst) in enumerate(((out_x, adjoint_hbm), (out_s, sens_hbm))):
                store = pltpu.make_async_copy(
                    src.at[:, here], dst.at[:, here], out_sem.at[m, g]
                )
                store.start()
                stores.append(store)

    for copies in started:
        for copy in copies:
            copy.wait_send()
    for store in stores:
        store.wait()


def deliver(adjoint, sens, adjoint_out, sens_out, sem):
    parts = sem.shape[1]
    span = adjoint.shape[0] // parts
    copies = []
    for n in range(parts):
        at = pl.ds(n * span, span)
        for m, (src, dst) in enumerate(((adjoint, adjoint_out), (sens, sens_out))):
            copies.append(pltpu.make_async_copy(src.at[at], dst.at[at], sem.at[m, n]))
    for copy in copies:
        copy.start()
    for copy in copies:
        copy.wait()


def solution(mesh):
    segments, sectors = mesh.shape["rad"], mesh.shape["azi"]
    spec = P("rad", "azi", None)

    def body(heat, size, flux, goal, start):
        rows, width, axial = heat.shape
        half_rows = width // 2
        tile_rows = half_rows * axial // (segments * LANES)
        block = pltpu.VMEM((rows, width, axial), jnp.float32)
        tile = (tile_rows, LANES)
        shape = jax.ShapeDtypeStruct((rows, width, axial), jnp.float32)
        dma = pltpu.SemaphoreType.DMA
        cells = rows * width * axial
        adjoint, sens = pl.pallas_call(
            functools.partial(kernel, segments, sectors),
            out_shape=(shape, shape),
            in_specs=[pl.BlockSpec(memory_space=pltpu.HBM)] * 5,
            out_specs=[pl.BlockSpec(memory_space=pl.ANY)] * 2,
            scratch_shapes=[block] * 12
            + [
                pltpu.VMEM((2, 2, rows, axial), jnp.float32),
                pltpu.VMEM((2, 2, rows, axial), jnp.float32),
                pltpu.VMEM((segments, 3, 2) + tile, jnp.float32),
                pltpu.VMEM((segments, 3, 2) + tile, jnp.float32),
                pltpu.VMEM((2, 2, segments, 2) + tile, jnp.float32),
                pltpu.VMEM((2, 2, segments, 2) + tile, jnp.float32),
                pltpu.VMEM((2, 2, segments, 2) + tile, jnp.float32),
                pltpu.VMEM((2, 2, segments, 2) + tile, jnp.float32),
                pltpu.VMEM((2, segments, 5) + tile, jnp.float32),
                pltpu.VMEM((2, half_rows, axial), jnp.float32),
                pltpu.VMEM((2, half_rows, axial), jnp.float32),
                dma((5, 2)),
                dma((2, width // SUB)),
                dma((2, 2)),
                dma((2, 2)),
                dma((segments,)),
                dma((segments,)),
                dma((2, 2, segments)),
                dma((2, 2, segments)),
                dma((2, 2, segments)),
                dma((2, 2, segments)),
            ],
            compiler_params=pltpu.CompilerParams(
                collective_id=0, has_side_effects=True, vmem_limit_bytes=51 * 2**20
            ),
            cost_estimate=pl.CostEstimate(
                flops=120 * cells, bytes_accessed=28 * cells, transcendentals=2 * cells
            ),
        )(heat, size, flux, goal, start)
        return pl.pallas_call(
            deliver,
            out_shape=(shape, shape),
            in_specs=[pl.BlockSpec(memory_space=pl.ANY)] * 2,
            out_specs=[pl.BlockSpec(memory_space=pl.ANY)] * 2,
            scratch_shapes=[dma((2, 4))],
            compiler_params=pltpu.CompilerParams(vmem_limit_bytes=2**20),
            cost_estimate=pl.CostEstimate(
                flops=0, bytes_accessed=16 * cells, transcendentals=0
            ),
        )(adjoint, sens)

    return jax.shard_map(
        body, mesh=mesh, in_specs=(spec,) * 5, out_specs=(spec, spec), check_vma=False
    )
```

profile of v0, /device:TPU:0, one launch (start us, length us, event | category | flops | bytes accessed | tf_op | source)
XLA Modules:
  0.0 28.6 jit_solution(17931627453793803657)
XLA Ops:
  0.6 26.6 %shard_map.68 = (f32[16,32,512]{2,1,0:T(8,128)S(1)}, f32[16,32,512]{2,1,0:T(8,128)S(1)}) custom-call(f32[16,32,512]{2,1,0:T(8,128)} %heat_hbm.1, f32[16,32,512]{2,1,0:T(8,128)} %size_hbm.1, f32[16,32,512]{2,1,0:T(8,128)} %flux_hbm.1, f32[16,32,512]{2,1,0:T(8,128)} %goal_hbm.1, f32[16,32,512]{2,1,0:T(8,128)} %start_hbm.1), custom_call_target="tpu_custom_call" | custom-call | flops 31457280 | bytes 7340032 | tf_op jit(solution)/shard_map/pallas_call | solution.py:541
  27.2 1.4 %shard_map.69 = (f32[16,32,512]{2,1,0:T(8,128)}, f32[16,32,512]{2,1,0:T(8,128)}) custom-call(f32[16,32,512]{2,1,0:T(8,128)S(1)} %get-tuple-element.4.adjoint, f32[16,32,512]{2,1,0:T(8,128)S(1)} %get-tuple-element.5.sens), custom_call_target="tpu_custom_call" | custom-call | bytes 4194304 | tf_op jit(solution)/shard_map/pallas_call | solution.py:577
where the time goes:
time: 28.7 us; the launch traced here: 28.6 us
  Pallas kernels  27.9 us (97%)
  between operations  0.64 us (2%)
    pallas_call x1, Pallas kernels, body(): pl.pallas_call(functools.partial(kernel, segments, sectors), out_shape=(s...  26.6 us
    pallas_call x1, Pallas kernels, body(): pl.pallas_call(deliver, out_shape=(shape, shape), in_specs=[pl.BlockSpec(...  1.38 us

commit v1 on v0

--- a/solution.py
+++ b/solution.py
@@ -436,11 +436,10 @@
     await_from(coef_out, coef_in, coef_ssem, coef_rsem)
     for half in (1, 0):
         reduced_factors(half)
-    for half in (1, 0):
-        substitute(half)
         await_ends(0, half)
         reduced_solve(0, half)
         started.append(send_back(0, half))
+        substitute(half)
 
     last_lane = lax.broadcasted_iota(jnp.int32, (width, axial), 1) == axial - 1
 
@@ -449,8 +448,6 @@
         rise = jnp.where(last_lane, 0.0, pltpu.roll(here, axial - 1, 1) - here)
         heat[i] = slope_weight * rise - size[i]
         return carry
-
-    lax.fori_loop(0, rows, slope, 0, unroll=4)
 
     for half in (1, 0):
         sides = ends(0, half)
@@ -471,20 +468,9 @@
             for copy in halos:
                 copy.start()
 
-    for half in (0, 1):
-        if half == 1:
-            for copy in halos:
-                copy.wait_recv()
-        right_side(1, half)
-        started.append(send_ends(1, half))
-    for half in (0, 1):
-        substitute(half)
-        await_ends(1, half)
-        reduced_solve(1, half)
-        started.append(send_back(1, half))
-
     stores = []
-    for half in (0, 1):
+
+    def finish_half(half):
         sides = ends(1, half)
 
         def finish(i, carry):
@@ -503,6 +489,25 @@
                 )
                 store.start()
                 stores.append(store)
+
+    def answer(half):
+        await_ends(1, half)
+        reduced_solve(1, half)
+        started.append(send_back(1, half))
+
+    right_side(1, 0)
+    started.append(send_ends(1, 0))
+    lax.fori_loop(0, rows, slope, 0, unroll=4)
+    answer(0)
+    for copy in halos:
+        copy.wait_recv()
+    right_side(1, 1)
+    started.append(send_ends(1, 1))
+    substitute(0)
+    substitute(1)
+    finish_half(0)
+    answer(1)
+    finish_half(1)
 
     for copies in started:
         for copy in copies:

time: 28.7 us -> 32 us (1.11)
  Pallas kernels: 27.9 us -> 31.3 us
    pallas_call x1, Pallas kernels: 26.6 us -> 29.9 us  [body(): pl.pallas_call(functools.partial(kernel, segments, sectors), out_shape=(s...]
where the time goes in v1:
time: 32 us; the launch traced here: 31.9 us
  Pallas kernels  31.3 us (98%)
  between operations  0.64 us (2%)
    pallas_call x1, Pallas kernels, body(): pl.pallas_call(functools.partial(kernel, segments, sectors), out_shape=(s...  29.9 us
    pallas_call x1, Pallas kernels, body(): pl.pallas_call(deliver, out_shape=(shape, shape), in_specs=[pl.BlockSpec(...  1.38 us

profile of v1, /device:TPU:0, one launch (start us, length us, event | category | flops | bytes accessed | tf_op | source)
XLA Modules:
  0.0 31.9 jit_solution(13691747763262879964)
XLA Ops:
  0.6 29.9 %shard_map.68 = (f32[16,32,512]{2,1,0:T(8,128)S(1)}, f32[16,32,512]{2,1,0:T(8,128)S(1)}) custom-call(f32[16,32,512]{2,1,0:T(8,128)} %heat_hbm.1, f32[16,32,512]{2,1,0:T(8,128)} %size_hbm.1, f32[16,32,512]{2,1,0:T(8,128)} %flux_hbm.1, f32[16,32,512]{2,1,0:T(8,128)} %goal_hbm.1, f32[16,32,512]{2,1,0:T(8,128)} %start_hbm.1), custom_call_target="tpu_custom_call" | custom-call | flops 31457280 | bytes 7340032 | tf_op jit(solution)/shard_map/pallas_call | solution.py:546
  30.5 1.4 %shard_map.69 = (f32[16,32,512]{2,1,0:T(8,128)}, f32[16,32,512]{2,1,0:T(8,128)}) custom-call(f32[16,32,512]{2,1,0:T(8,128)S(1)} %get-tuple-element.4.adjoint, f32[16,32,512]{2,1,0:T(8,128)S(1)} %get-tuple-element.5.sens), custom_call_target="tpu_custom_call" | custom-call | bytes 4194304 | tf_op jit(solution)/shard_map/pallas_call | solution.py:582

commit v2 on v0

--- a/solution.py
+++ b/solution.py
@@ -29,8 +29,8 @@
     flux_hbm,
     goal_hbm,
     start_hbm,
-    adjoint_hbm,
-    sens_hbm,
+    out_x,
+    out_s,
     heat,
     size,
     flux,
@@ -41,8 +41,6 @@
     rb,
     rhs,
     part,
-    out_x,
-    out_s,
     halo_out,
     halo_in,
     coef_out,
@@ -55,7 +53,6 @@
     side_a,
     side_b,
     in_sem,
-    out_sem,
     halo_ssem,
     halo_rsem,
     coef_ssem,
@@ -483,7 +480,6 @@
         reduced_solve(1, half)
         started.append(send_back(1, half))
 
-    stores = []
     for half in (0, 1):
         sides = ends(1, half)
 
@@ -495,20 +491,9 @@
             return carry
 
         lax.fori_loop(0, rows, finish, 0, unroll=4)
-        for g in halves[half]:
-            here = pl.ds(g * SUB, SUB)
-            for m, (src, dst) in enumerate(((out_x, adjoint_hbm), (out_s, sens_hbm))):
-                store = pltpu.make_async_copy(
-                    src.at[:, here], dst.at[:, here], out_sem.at[m, g]
-                )
-                store.start()
-                stores.append(store)
-
     for copies in started:
         for copy in copies:
             copy.wait_send()
-    for store in stores:
-        store.wait()
 
 
 def deliver(adjoint, sens, adjoint_out, sens_out, sem):
@@ -542,8 +527,8 @@
             functools.partial(kernel, segments, sectors),
             out_shape=(shape, shape),
             in_specs=[pl.BlockSpec(memory_space=pltpu.HBM)] * 5,
-            out_specs=[pl.BlockSpec(memory_space=pl.ANY)] * 2,
-            scratch_shapes=[block] * 12
+            out_specs=[pl.BlockSpec(memory_space=pltpu.VMEM)] * 2,
+            scratch_shapes=[block] * 10
             + [
                 pltpu.VMEM((2, 2, rows, axial), jnp.float32),
                 pltpu.VMEM((2, 2, rows, axial), jnp.float32),
@@ -557,7 +542,6 @@
                 pltpu.VMEM((2, half_rows, axial), jnp.float32),
                 pltpu.VMEM((2, half_rows, axial), jnp.float32),
                 dma((5, 2)),
-                dma((2, width // SUB)),
                 dma((2, 2)),
                 dma((2, 2)),
                 dma((segments,)),

time: 28.7 us -> 28.6 us (level)
  no operation moved by 1% of the time
where the time goes in v2:
time: 28.6 us; the launch traced here: 28.4 us
  Pallas kernels  27.8 us (97%)
  between operations  0.64 us (2%)
    pallas_call x1, Pallas kernels, body(): pl.pallas_call(functools.partial(kernel, segments, sectors), out_shape=(s...  26.4 us
    pallas_call x1, Pallas kernels, body(): pl.pallas_call(deliver, out_shape=(shape, shape), in_specs=[pl.BlockSpec(...  1.38 us

profile of v2, /device:TPU:0, one launch (start us, length us, event | category | flops | bytes accessed | tf_op | source)
XLA Modules:
  0.0 28.4 jit_solution(16705316340209566442)
XLA Ops:
  0.6 26.4 %shard_map.68 = (f32[16,32,512]{2,1,0:T(8,128)S(1)}, f32[16,32,512]{2,1,0:T(8,128)S(1)}) custom-call(f32[16,32,512]{2,1,0:T(8,128)} %heat_hbm.1, f32[16,32,512]{2,1,0:T(8,128)} %size_hbm.1, f32[16,32,512]{2,1,0:T(8,128)} %flux_hbm.1, f32[16,32,512]{2,1,0:T(8,128)} %goal_hbm.1, f32[16,32,512]{2,1,0:T(8,128)} %start_hbm.1), custom_call_target="tpu_custom_call" | custom-call | flops 31457280 | bytes 7340032 | tf_op jit(solution)/shard_map/pallas_call | solution.py:526
  27.0 1.4 %shard_map.69 = (f32[16,32,512]{2,1,0:T(8,128)}, f32[16,32,512]{2,1,0:T(8,128)}) custom-call(f32[16,32,512]{2,1,0:T(8,128)S(1)} %get-tuple-element.4.adjoint, f32[16,32,512]{2,1,0:T(8,128)S(1)} %get-tuple-element.5.sens), custom_call_target="tpu_custom_call" | custom-call | bytes 4194304 | tf_op jit(solution)/shard_map/pallas_call | solution.py:561
